TPU v7x, 32 devices: a whole 2x2x4 slice. The times are simulated.
32 devices in a mesh: seq: 4 (over y, core), head: 8 (over z, x).
Axes of the slice: x: 2, y: 2, z: 4, core: 2. Of those that a mesh axis runs over, the one named last changes fastest.
Arguments:
- query_latent: bfloat16 [1024, 128, 576], P('seq', 'head'), may hold values from -6 to 6
- key_latent: bfloat16 [512, 576], P('seq'), may hold values from -6 to 6
- normalizer: float32 [1024, 128], P('seq', 'head'), may hold values from 7 to 9
- index_query: bfloat16 [1024, 64, 128], P('seq', 'head'), may hold values from -20 to 20
- index_key: bfloat16 [512, 128], P('seq'), may hold values from -6.5 to 6.5
- index_weight: float32 [1024, 64], P('seq', 'head'), may hold values from 0.05 to 0.5
- kept: int32 [8, 4], P('seq'), may hold values from 0 to 1, as said below
Outputs:
- index_query_grad: bfloat16 [1024, 64, 128], P('seq', 'head')
- index_key_grad: float32 [512, 128], P('seq')
Inputs may be any that keep to these rules, and one draw needn't show every extreme that they name: `kept`: every query tile keeps the key tile whose position matches its own block of 256 queries.
All inputs are finite; a program needn't handle non-finite values.
Results may differ from a plain program's by a relative error of at most 0.009.
Values may be sent and summed in bfloat16 or wider, within the bound.
A program may use at most 64 MiB of HBM per device.

v0:
```python
import jax
import jax.numpy as jnp
from jax import lax
from jax.sharding import PartitionSpec as P

attn_scale = 192.0 ** (-0.5)


def logit_gradient(head_sum, logit, keep):
    target = head_sum / jnp.sum(head_sum, axis=1, keepdims=True)
    top = jnp.max(jnp.where(keep, logit, -jnp.inf), axis=1, keepdims=True)
    expo = jnp.where(keep, jnp.exp(jnp.where(keep, logit, top) - top), 0.0)
    return expo / jnp.sum(expo, axis=1, keepdims=True) - target


def local(query_latent, key_latent, normalizer, index_query, index_key, index_weight, kept):
    query_rows, head_count, width = query_latent.shape
    tile_rows = index_key.shape[0]
    index_scale = index_query.shape[2] ** (-0.5)
    keys_whole = lax.all_gather(index_key, "seq", axis=0, tiled=True)
    allow = jnp.repeat(jnp.repeat(kept, tile_rows, axis=0), tile_rows, axis=1) > 0
    z_val = (
        jnp.einsum("tjd,sd->tjs", index_query, keys_whole, preferred_element_type=jnp.float32)
        * index_scale
    )
    logit_part = jnp.sum(index_weight[:, :, None] * jnp.maximum(z_val, 0.0), axis=1)
    flat_query = query_latent.reshape(query_rows * head_count, width)
    piece = lax.all_gather(key_latent, "seq", axis=0, tiled=True)
    count = piece.shape[0]
    scores = (
        jnp.einsum("rc,sc->rs", flat_query, piece, preferred_element_type=jnp.float32) * attn_scale
    )
    prob = jnp.exp(scores.reshape(query_rows, head_count, count) - normalizer[:, :, None])
    partial_value = jnp.where(allow, jnp.sum(prob, axis=1), 0.0)
    head_sum, logit = lax.psum((partial_value, logit_part), "head")
    gradient = logit_gradient(head_sum, logit, allow)
    dz_val = jnp.where(z_val > 0, gradient[:, None, :] * index_weight[:, :, None], 0.0).astype(
        jnp.bfloat16
    )
    dquery = (
        jnp.einsum("tjs,sd->tjd", dz_val, keys_whole, preferred_element_type=jnp.float32)
        * index_scale
    ).astype(jnp.bfloat16)
    dkey = lax.psum_scatter(
        (
            jnp.einsum("tjs,tjd->sd", dz_val, index_query, preferred_element_type=jnp.float32)
            * index_scale
        ).astype(jnp.bfloat16),
        "seq",
        scatter_dimension=0,
        tiled=True,
    ).astype(jnp.float32)
    dkey = lax.psum(dkey.astype(jnp.bfloat16), "head").astype(jnp.float32)
    return (dquery, dkey)


def solution(mesh):
    return jax.shard_map(
        local,
        mesh=mesh,
        in_specs=(
            P("seq", "head", None),
            P("seq", None),
            P("seq", "head"),
            P("seq", "head", None),
            P("seq", None),
            P("seq", "head"),
            P("seq", None),
        ),
        out_specs=(P("seq", "head", None), P("seq", None)),
        check_vma=False,
    )
```

profile of v0, /device:TPU:0, one launch (start us, length us, event | category | flops | bytes accessed | tf_op | source)
XLA Modules:
  0.0 194.7 jit_solution(13626170334361925491)
XLA Ops:
  7.2 0.0 all-reduce.3.cloned.1.call-start
  7.2 0.8 copy.16
  8.0 0.0 copy-start.1
  8.0 0.0 copy-start.4
  8.0 0.0 copy-start.2
  8.1 9.0 %copy.15 = bf16[256,16,576]{2,1,0:T(8,128)(2,1)} copy(bf16[256,16,576]{0,2,1:T(8,128)(2,1)} %param.7) | data formatting | bytes 9437184 | tf_op args[0]
  17.1 0.0 copy-done.1
  17.1 9.0 %all_gather.7 = bf16[512,576]{0,1:T(8,128)(2,1)S(1)} all-gather(bf16[128,576]{0,1:T(8,128)(2,1)S(1)} %copy-done.1), channel_id=1, replica_groups=mesh['seq'=4,'head'=8] {'seq'}, dimensions={0}, use_global_device_ids=true | all-gather | bytes 737280 | tf_op jit(solution)/shard_map/all_gather | solution.py:28
  26.1 0.0 copy-done.4
  26.1 0.0 copy-done.2
  26.1 5.4 %all_gather.6 = bf16[512,128]{1,0:T(8,128)(2,1)S(1)} all-gather(bf16[128,128]{1,0:T(8,128)(2,1)S(1)} %copy-done.2), channel_id=1, replica_groups=mesh['seq'=4,'head'=8] {'seq'}, dimensions={0}, use_global_device_ids=true | all-gather | bytes 163840 | tf_op jit(solution)/shard_map/all_gather | solution.py:20
  31.5 0.0 copy-start
  31.5 0.0 copy-start.3
  31.5 7.5 %exponential_reduce_fusion = f32[256,512]{1,0:T(8,128)S(1)} fusion(f32[256,16]{1,0:T(8,128)S(1)} %copy.16, bf16[4096,576]{1,0:T(8,128)(2,1)} %bitcast.28, bf16[512,576]{0,1:T(8,128)(2,1)S(1)} %all_gather.7), kind=kOutput, calls=%fused_computation | convolution fusion | flops 2422079488 | bytes 5849088 | tf_op jit(solution)/shard_map/rc,sc->rs/dot_general | solution.py:31
  39.0 0.3 broadcast_in_dim.32
  39.3 0.9 bitcast_select_fusion
  40.2 0.0 copy-done
  40.2 0.0 copy-done.3
  40.2 3.6 %multiply_reduce_fusion = (f32[256,512]{1,0:T(8,128)}, f32[256,8,512]{2,0,1:T(8,128)}) fusion(f32[256,8]{0,1:T(8,128)S(1)} %copy-done.3, bf16[512,128]{1,0:T(8,128)(2,1)S(1)} %all_gather.6, bf16[256,8,128]{2,1,0:T(8,128)(2,1)S(1)} %copy-done), kind=kOutput, calls=%fused_computation.5 | convolution fusion | flops 272498688 | bytes 5382144 | tf_op jit(solution)/shard_map/tjd,sd->tjs/dot_general | solution.py:23
  43.8 0.0 all-reduce.3.cloned.1.call-update
  43.8 0.0 reduce-scatter.2.cloned.1.call-start
  43.9 2.9 %fusion.15 = u8[256,512]{1,0:T(8,128)(4,1)S(1)} fusion(f32[256,8,512]{2,0,1:T(8,128)} %get-tuple-element.9), kind=kLoop, calls=%fused_computation.21 | loop fusion | flops 6160384 | bytes 4325376
  46.8 76.5 %all-reduce.3.cloned.1.call-done = (f32[256,512]{1,0:T(8,128)}, f32[256,512]{1,0:T(8,128)}) async-done(((f32[256,512]{1,0:T(8,128)}, f32[256,512]{1,0:T(8,128)}), (f32[256,512]{1,0:T(8,128)}, f32[256,512]{1,0:T(8,128)})) %all-reduce.3.cloned.1.call-update) | async-done | bytes 1048592 | tf_op jit(solution)/shard_map/psum | solution.py:35
  123.3 1.2 select_reduce_fusion
  124.5 1.3 fusion.21
  125.8 1.2 reduce_sum.39
  127.0 1.5 divide_subtract_fusion
  128.4 1.9 fusion.14
  130.3 0.0 reduce-scatter.2.cloned.1.call-update
  130.3 0.9 fusion.11
  131.3 1.1 copy.19
  132.4 17.1 %reduce-scatter.2.cloned.1.call-done = bf16[128,128]{1,0:T(8,128)(2,1)} async-done(((bf16[512,128]{1,0:T(8,128)(2,1)}), bf16[128,128]{1,0:T(8,128)(2,1)}) %reduce-scatter.2.cloned.1.call-update) | async-done | bytes 32784 | tf_op jit(solution)/shard_map/reduce_scatter | solution.py:44
  149.5 37.7 %psum.23 = bf16[128,128]{1,0:T(8,128)(2,1)S(1)} all-reduce(bf16[128,128]{1,0:T(8,128)(2,1)} %reduce-scatter.2.cloned.1.call-done), channel_id=1, replica_groups=mesh['seq'=4,'head'=8] {'head'}, use_global_device_ids=true, to_apply=%region_8.9 | all-reduce | flops 16384 | bytes 65536 | tf_op jit(solution)/shard_map/psum | solution.py:53
  187.2 0.6 convert_element_type.17
  (2 shorter events, 0.0 us)
Async XLA Ops:
  7.2 116.1 %all-reduce.3.cloned.1.call-start = ((), (), s32[]{:S(2)}) async-start(), calls=%async_computation.2 | async-start | bytes 2097152 | tf_op jit(solution)/shard_map/psum | solution.py:35
  8.0 9.0 %copy-start.1 = (bf16[128,576]{0,1:T(8,128)(2,1)S(1)}, bf16[128,576]{0,1:T(8,128)(2,1)}, u32[]{:S(2)}) copy-start(bf16[128,576]{0,1:T(8,128)(2,1)} %param.8) | copy-start | bytes 442372
  8.0 18.0 %copy-start.4 = (s32[2,4]{1,0:T(2,128)S(1)}, s32[2,4]{1,0:T(2,128)}, u32[]{:S(2)}) copy-start(s32[2,4]{1,0:T(2,128)} %param.13) | copy-start | bytes 100
  8.0 18.0 %copy-start.2 = (bf16[128,128]{1,0:T(8,128)(2,1)S(1)}, bf16[128,128]{1,0:T(8,128)(2,1)}, u32[]{:S(2)}) copy-start(bf16[128,128]{1,0:T(8,128)(2,1)} %param.11) | copy-start | bytes 98308
  31.5 8.7 %copy-start = (bf16[256,8,128]{2,1,0:T(8,128)(2,1)S(1)}, bf16[256,8,128]{2,1,0:T(8,128)(2,1)}, u32[]{:S(2)}) copy-start(bf16[256,8,128]{2,1,0:T(8,128)(2,1)} %param.10) | copy-start | bytes 1572868
  31.5 8.7 %copy-start.3 = (f32[256,8]{0,1:T(8,128)S(1)}, f32[256,8]{0,1:T(8,128)}, u32[]{:S(2)}) copy-start(f32[256,8]{0,1:T(8,128)} %param.12) | copy-start | bytes 24580
  43.8 105.6 %reduce-scatter.2.cloned.1.call-start = ((), (), s32[]{:S(2)}) async-start(), calls=%async_computation.1 | async-start | bytes 163840 | tf_op jit(solution)/shard_map/reduce_scatter | solution.py:44
Sparse Core Ops, SparseCore 0:
  44.0 79.2 all-reduce.2
  130.5 18.9 reduce-scatter.1
where the time goes:
time: 195 us
  waiting for transfers between devices  93.6 us (48%)
  blocking collectives  52.2 us (27%)
  between operations  14.1 us (7%)
  matrix products  13.9 us (7%)
  local copies, waits for them, and re-layouts  11.3 us (6%)
  other arithmetic  9.55 us (5%)
    psum x1, waiting for transfers between devices, local(): head_sum, logit = lax.psum((partial_value, logit_part), 'head')  76.5 us
    psum x1, blocking collectives, local(): dkey = lax.psum(dkey.astype(jnp.bfloat16), 'head').astype(jnp.float32)  37.7 us
    reduce_scatter x1, waiting for transfers between devices, local(): lax.psum_scatter((jnp.einsum('tjs,tjd->sd', dz_val, index_query, preferre...  17.1 us
    unnamed x13, local copies, waits for them, and re-layouts  11 us
    all_gather x1, blocking collectives, local(): piece = lax.all_gather(key_latent, 'seq', axis=0, tiled=True)  8.99 us
    dot_general x1, matrix products, local(): jnp.einsum('rc,sc->rs', flat_query, piece, preferred_element_type=jnp.flo...  7.47 us
    all_gather x1, blocking collectives, local(): keys_whole = lax.all_gather(index_key, 'seq', axis=0, tiled=True)  5.43 us
  transfers between devices with their start and end apart: 2, of which 2 were waited for; matrix products, arithmetic and copies ran while one was open for 3% of the time, Pallas kernels for 0%

commit v1 on v0

v1 whole, which is shorter than its diff:
```python
import functools
import jax
import jax.numpy as jnp
from jax import lax
from jax.experimental import pallas as pl
from jax.experimental.pallas import tpu as pltpu
from jax.sharding import PartitionSpec as P

attn_scale = 192.0 ** (-0.5)
MESH = pl.DeviceIdType.MESH
F32 = jnp.float32
BF16 = jnp.bfloat16


def dot(a, b, ca, cb):
    return lax.dot_general(a, b, (((ca,), (cb,)), ((), ())), preferred_element_type=F32)


def column(ref_rows, heads):
    rows = ref_rows.shape[0]
    wide = jnp.broadcast_to(ref_rows[:, None, :], (rows, heads, heads))
    sub = lax.broadcasted_iota(jnp.int32, (rows, heads, heads), 1)
    lane = lax.broadcasted_iota(jnp.int32, (rows, heads, heads), 2)
    return jnp.sum(jnp.where(sub == lane, wide, 0.0), axis=2, keepdims=True)


def kernel(
    ns, nh, heads, iheads, index_scale,
    q_hbm, kl_ref, nrm_ref, iq_ref, ik_ref, w_ref, kept_ref,
    dq_ref, dk_ref,
    qbuf, klat, keys, wm,
    s1l, s1h, r1l, r1h, s2l, s2h, r2l, r2h, gall, acc,
    sa, ra, sb, rb, rc,
    q_sem, ik_send, ik_recv, kl_send, kl_recv,
    l1_send, l1_recv, h1_send, h1_recv, l2_send, l2_recv, h2_send, h2_recv,
    g_send, g_fsend, g_recv, a_send, a_recv, b_send, b_recv, c_send, c_recv,
):
    me_s, me_h = lax.axis_index("seq"), lax.axis_index("head")
    half = nh // 2
    mz, mx = me_h // 2, me_h % 2
    px = 1 - mx
    pair = mz * 2 + px
    n_keys, kb = klat.shape[0], kl_ref.shape[0]
    cr = r1l.shape[1]
    qr, wr = cr * heads, cr * iheads

    def chunk_of(i):
        first = i < half
        zt = (mz + 1 + i) % half
        return zt, jnp.where(first, px, mx) * half + zt

    def copy(src, dst, ss, rs, s, h):
        return pltpu.make_async_remote_copy(
            src_ref=src, dst_ref=dst, send_sem=ss, recv_sem=rs,
            device_id=(s, h), device_id_type=MESH,
        )

    def q_copy(i):
        _, k = chunk_of(i)
        return pltpu.make_async_copy(q_hbm.at[pl.ds(k * qr, qr)], qbuf.at[i], q_sem.at[i])

    for i in range(nh):
        q_copy(i).start()

    barrier = pltpu.get_barrier_semaphore()
    for d in range(1, ns):
        pl.semaphore_signal(barrier, inc=1, device_id=((me_s + d) % ns, me_h), device_id_type=MESH)
    for d in range(1, nh):
        pl.semaphore_signal(barrier, inc=1, device_id=(me_s, (me_h + d) % nh), device_id_type=MESH)
    pl.semaphore_wait(barrier, ns - 1 + nh - 1)

    def own_rows(s):
        return pl.ds(pl.multiple_of(s * kb, kb), kb)

    def ik_copy(d, s):
        return copy(ik_ref, keys.at[own_rows(s)], ik_send.at[d], ik_recv.at[s], (me_s + d) % ns, me_h)

    def kl_copy(d, s):
        return copy(kl_ref, klat.at[own_rows(s)], kl_send.at[d], kl_recv.at[s], (me_s + d) % ns, me_h)

    for d in range(1, ns):
        ik_copy(d, me_s).start()
    for d in range(1, ns):
        kl_copy(d, me_s).start()
    keys[own_rows(me_s), :] = ik_ref[...]
    klat[own_rows(me_s), :] = kl_ref[...]
    for d in range(1, ns):
        ik_copy(d, (me_s + d) % ns).wait_recv()
    for d in range(1, ns):
        kl_copy(d, (me_s + d) % ns).wait_recv()

    def l1_copy(zt):
        return copy(s1l.at[zt], r1l.at[zt], l1_send.at[zt], l1_recv.at[zt], me_s, pair)

    def h1_copy(zt):
        return copy(s1h.at[zt], r1h.at[zt], h1_send.at[zt], h1_recv.at[zt], me_s, pair)

    def l2_copy(zt, frm):
        return copy(s2l.at[zt], r2l.at[frm], l2_send.at[zt], l2_recv.at[frm], me_s, zt * 2 + mx)

    def h2_copy(zt, frm):
        return copy(s2h.at[zt], r2h.at[frm], h2_send.at[zt], h2_recv.at[frm], me_s, zt * 2 + mx)

    def step(i, _):
        zt, k = chunk_of(i)
        rows = pl.ds(pl.multiple_of(k * cr, cr), cr)
        wide = pl.ds(pl.multiple_of(k * wr, wr), wr)
        z = dot(iq_ref[wide, :], keys[...], 1, 1).reshape(cr, iheads, n_keys)
        part = jnp.where(z > 0, column(w_ref[rows, :], iheads), 0.0)
        wm[k] = part.reshape(wr, n_keys)
        logit = jnp.sum(part * z, axis=1) * index_scale

        @pl.when(i < half)
        def _():
            s1l[zt] = logit
            l1_copy(zt).start()

        q_copy(i).wait()
        scores = dot(qbuf[i], klat[...], 1, 1).reshape(cr, heads, n_keys)
        prob = jnp.exp(scores * attn_scale - column(nrm_ref[rows, :], heads))
        value = jnp.sum(prob, axis=1)

        @pl.when(i < half)
        def _():
            s1h[zt] = value.astype(BF16)
            h1_copy(zt).start()

        @pl.when(i >= half)
        def _():
            l1_copy(zt).wait_recv()
            s2l[zt] = logit + r1l[zt]

            @pl.when(i < nh - 1)
            def _():
                l2_copy(zt, mz).start()

            h1_copy(zt).wait_recv()
            s2h[zt] = (value + r1h[zt].astype(F32)).astype(BF16)

            @pl.when(i < nh - 1)
            def _():
                h2_copy(zt, mz).start()

        return 0

    lax.fori_loop(0, nh, step, 0)

    logit = s2l[mz]
    head_sum = s2h[mz].astype(F32)
    for d in range(1, half):
        frm = (mz + half - d) % half
        l2_copy(frm, frm).wait_recv()
        logit = logit + r2l[frm]
    for d in range(1, half):
        frm = (mz + half - d) % half
        h2_copy(frm, frm).wait_recv()
        head_sum = head_sum + r2h[frm].astype(F32)

    mine = mx * half + mz
    tile_rows = (cr * nh) // kept_ref.shape[0]
    tile_at = (mine * cr) // tile_rows
    kt = n_keys // kept_ref.shape[1]
    keep = jnp.concatenate(
        [jnp.full((cr, kt), kept_ref[tile_at, j], jnp.int32) for j in range(kept_ref.shape[1])],
        axis=1,
    ) > 0
    head_sum = jnp.where(keep, head_sum, 0.0)
    target = head_sum / jnp.sum(head_sum, axis=1, keepdims=True)
    top = jnp.max(jnp.where(keep, logit, -jnp.inf), axis=1, keepdims=True)
    expo = jnp.where(keep, jnp.exp(jnp.where(keep, logit, top) - top), 0.0)
    gall[mine] = (expo / jnp.sum(expo, axis=1, keepdims=True) - target).astype(BF16)

    def g_copy(d, k):
        zt = (mz + d) % half
        return copy(gall.at[k], gall.at[k], g_send.at[d], g_recv.at[k], me_s, zt * 2 + mx)

    def g_pass(d, k):
        return copy(gall.at[k], gall.at[k], g_fsend.at[d], g_recv.at[k], me_s, pair)

    for d in range(1, half):
        g_copy(d, mine).start()
    g_pass(0, mine).start()

    acc[...] = jnp.zeros_like(acc)

    def backward(k):
        wide = pl.ds(pl.multiple_of(k * wr, wr), wr)
        g = gall[k].astype(F32)
        dz = (g[:, None, :] * wm[k].reshape(cr, iheads, n_keys)).astype(BF16).reshape(wr, n_keys)
        dq_ref[wide, :] = (dot(dz, keys[...], 1, 0) * index_scale).astype(BF16)
        acc[...] += dot(iq_ref[wide, :], dz, 0, 0)

    def back_step(i, _):
        zt = (mz + half - i % half) % half
        k = jnp.where(i < half, mx, px) * half + zt

        @pl.when(jnp.logical_and(i > 0, i < half))
        def _():
            g_copy(i, k).wait_recv()
            g_pass(i, k).start()

        @pl.when(i >= half)
        def _():
            g_pass(i - half, k).wait_recv()

        backward(k)
        return 0

    lax.fori_loop(0, nh, back_step, 0)

    wire = sb.dtype
    br = rb.shape[1]

    def a_copy(d, s):
        return copy(sa.at[d], ra.at[s], a_send.at[d], a_recv.at[s], (me_s + d) % ns, me_h)

    for d in range(1, ns):
        sa[d] = (acc[:, own_rows((me_s + d) % ns)] * index_scale).astype(BF16)
        a_copy(d, me_s).start()
    total = acc[:, own_rows(me_s)] * index_scale
    for d in range(1, ns):
        a_copy(d, (me_s + d) % ns).wait_recv()
        total = total + ra[(me_s + d) % ns].astype(F32)
    sb[...] = total.astype(wire)

    def b_rows(h):
        return pl.ds(pl.multiple_of(h * br, br), br)

    def b_copy(d, h):
        to = (me_h + d) % nh
        return copy(sb.at[b_rows(to)], rb.at[h], b_send.at[d], b_recv.at[h], me_s, to)

    def c_copy(d, h):
        return copy(rc.at[b_rows(h)], rc.at[b_rows(h)], c_send.at[d], c_recv.at[h], me_s, (me_h + d) % nh)

    for d in range(1, nh):
        b_copy(d, me_h).start()
    piece = sb[b_rows(me_h), :].astype(F32)
    for d in range(1, nh):
        frm = (me_h + d) % nh
        b_copy(d, frm).wait_recv()
        piece = piece + rb[frm].astype(F32)
    rc[b_rows(me_h), :] = piece.astype(wire)
    for d in range(1, nh):
        c_copy(d, me_h).start()
    for d in range(1, nh):
        c_copy(d, (me_h + d) % nh).wait_recv()
    dk_ref[...] = rc[...].astype(F32).T

    for d in range(1, ns):
        ik_copy(d, me_s).wait_send()
        kl_copy(d, me_s).wait_send()
        a_copy(d, me_s).wait_send()
    for i in range(half):
        l1_copy(i).wait_send()
        h1_copy(i).wait_send()
        g_pass(i, mine).wait_send()
    for d in range(1, half):
        zt = (mz + d) % half
        l2_copy(zt, mz).wait_send()
        h2_copy(zt, mz).wait_send()
        g_copy(d, mine).wait_send()
    for d in range(1, nh):
        b_copy(d, me_h).wait_send()
        c_copy(d, me_h).wait_send()


def local(ns, nh, query_latent, key_latent, normalizer, index_query, index_key, index_weight, kept):
    t, heads, width = query_latent.shape
    ihead, idim = index_query.shape[1:]
    iheads = -(-ihead // 8) * 8
    if iheads != ihead:
        index_query = jnp.pad(index_query, ((0, 0), (0, iheads - ihead), (0, 0)))
        index_weight = jnp.pad(index_weight, ((0, 0), (0, iheads - ihead)))
    kb = key_latent.shape[0]
    n_keys = kb * ns
    cr, half, br = t // nh, nh // 2, idim // nh
    wire = BF16 if br % 16 == 0 else F32
    vmem, dma = pltpu.VMEM, pltpu.SemaphoreType.DMA
    in_vmem = pl.BlockSpec(memory_space=pltpu.VMEM)
    dq, dk = pl.pallas_call(
        functools.partial(kernel, ns, nh, heads, iheads, idim ** (-0.5)),
        out_shape=(
            jax.ShapeDtypeStruct((t * iheads, idim), BF16),
            jax.ShapeDtypeStruct((kb, idim), F32),
        ),
        in_specs=[pl.BlockSpec(memory_space=pl.ANY)] + [in_vmem] * 5
        + [pl.BlockSpec(memory_space=pltpu.SMEM)],
        out_specs=(in_vmem, in_vmem),
        scratch_shapes=[
            vmem((nh, cr * heads, width), BF16),
            vmem((n_keys, width), BF16),
            vmem((n_keys, idim), BF16),
            vmem((nh, cr * iheads, n_keys), F32),
            vmem((half, cr, n_keys), F32),
            vmem((half, cr, n_keys), BF16),
            vmem((half, cr, n_keys), F32),
            vmem((half, cr, n_keys), BF16),
            vmem((half, cr, n_keys), F32),
            vmem((half, cr, n_keys), BF16),
            vmem((half, cr, n_keys), F32),
            vmem((half, cr, n_keys), BF16),
            vmem((nh, cr, n_keys), BF16),
            vmem((idim, n_keys), F32),
            vmem((ns, idim, kb), BF16),
            vmem((ns, idim, kb), BF16),
            vmem((idim, kb), wire),
            vmem((nh, br, kb), wire),
            vmem((idim, kb), wire),
            dma((nh,)), dma((ns,)), dma((ns,)), dma((ns,)), dma((ns,)),
            dma((half,)), dma((half,)), dma((half,)), dma((half,)),
            dma((half,)), dma((half,)), dma((half,)), dma((half,)),
            dma((half,)), dma((half,)), dma((nh,)),
            dma((ns,)), dma((ns,)), dma((nh,)), dma((nh,)), dma((nh,)), dma((nh,)),
        ],
        compiler_params=pltpu.CompilerParams(
            collective_id=0, has_side_effects=True, vmem_limit_bytes=56 * 1024 * 1024
        ),
    )(
        query_latent.reshape(t * heads, width), key_latent, normalizer,
        index_query.reshape(t * iheads, idim), index_key, index_weight, kept,
    )
    dq = dq.reshape(t, iheads, idim)
    return (dq[:, :ihead] if iheads != ihead else dq), dk


def solution(mesh):
    ns, nh = mesh.shape["seq"], mesh.shape["head"]
    return jax.shard_map(
        functools.partial(local, ns, nh),
        mesh=mesh,
        in_specs=(
            P("seq", "head", None),
            P("seq", None),
            P("seq", "head"),
            P("seq", "head", None),
            P("seq", None),
            P("seq", "head"),
            P("seq", None),
        ),
        out_specs=(P("seq", "head", None), P("seq", None)),
        check_vma=False,
    )
```

time: 195 us -> 69.2 us (0.35)
  waiting for transfers between devices: 93.6 us -> 0 us
  blocking collectives: 52.2 us -> 0 us
  Pallas kernels: 0 us -> 51.2 us
  matrix products: 13.9 us -> 0 us
  between operations: 14.1 us -> 0.64 us
  other arithmetic: 9.55 us -> 0 us
  local copies, waits for them, and re-layouts: 11.3 us -> 16.9 us
    psum x1 -> x0, waiting for transfers between devices: 76.5 us -> none  [local(): head_sum, logit = lax.psum((partial_value, logit_part), 'head')]
    pallas_call x0 -> x1, Pallas kernels: none -> 51.2 us  [local(): pl.pallas_call(functools.partial(kernel, ns, nh, heads, iheads, idim ** (...]
    psum x1 -> x0, blocking collectives: 37.7 us -> none  [local(): dkey = lax.psum(dkey.astype(jnp.bfloat16), 'head').astype(jnp.float32)]
    reduce_scatter x1 -> x0, waiting for transfers between devices: 17.1 us -> none  [local(): lax.psum_scatter((jnp.einsum('tjs,tjd->sd', dz_val, index_query, preferre...]
    all_gather x2 -> x0, blocking collectives: 14.4 us -> none  [the longest x1 8.99 us: local(): piece = lax.all_gather(key_latent, 'seq', axis=0, tiled=True)]
    dot_general x4 -> x0, matrix products: 13.9 us -> none  [the longest x1 7.47 us: local(): jnp.einsum('rc,sc->rs', flat_query, piece, preferred_element_type=jnp.flo...]
    unnamed x13 -> x6, local copies, waits for them, and re-layouts: 11 us -> 16.9 us
    unnamed x1 -> x0, other arithmetic: 2.9 us -> none
  transfers between devices with their start and end apart: 2 -> 0, of which waited for: 2 -> 0; matrix products, arithmetic and copies ran while one was open for 3% -> 0% of each run, Pallas kernels for 0% -> 0%
where the time goes in v1:
time: 69.2 us; the launch traced here: 68.7 us
  Pallas kernels  51.2 us (74%)
  local copies, waits for them, and re-layouts  16.9 us (24%)
    pallas_call x1, Pallas kernels, local(): pl.pallas_call(functools.partial(kernel, ns, nh, heads, iheads, idim ** (...  51.2 us
    unnamed x6, local copies, waits for them, and re-layouts  16.9 us

profile of v1, /device:TPU:0, one launch (start us, length us, event | category | flops | bytes accessed | tf_op | source)
XLA Modules:
  0.0 68.7 jit_solution(11776619950906971170)
XLA Ops:
  0.6 1.5 %copy.11.nrm_ref = f32[256,16]{1,0:T(8,128)} copy(f32[256,16]{0,1:T(8,128)} %param.9) | data formatting | bytes 32768 | tf_op args[2]
  2.1 1.5 %copy.12.w_ref = f32[256,8]{1,0:T(8,128)} copy(f32[256,8]{0,1:T(8,128)} %param.12) | data formatting | bytes 16384 | tf_op args[5]
  3.6 1.7 %copy.10.kl_ref = bf16[128,576]{1,0:T(8,128)(2,1)} copy(bf16[128,576]{0,1:T(8,128)(2,1)} %param.8) | data formatting | bytes 294912 | tf_op args[1]
  5.3 8.9 %copy.9 = bf16[256,16,576]{2,1,0:T(8,128)(2,1)} copy(bf16[256,16,576]{0,2,1:T(8,128)(2,1)} %param.7) | data formatting | bytes 9437184 | tf_op args[0]
  14.2 51.2 %shard_map.86 = (bf16[2048,128]{1,0:T(8,128)(2,1)}, f32[128,128]{1,0:T(8,128)}) custom-call(bf16[4096,576]{1,0:T(8,128)(2,1)} %bitcast.3, bf16[128,576]{1,0:T(8,128)(2,1)} %copy.10.kl_ref, f32[256,16]{1,0:T(8,128)} %copy.11.nrm_ref, bf16[2048,128]{1,0:T(8,128)(2,1)} %bitcast.4, bf16[128,128]{1,0:T(8,128)(2,1)} %ik_ref.1, f32[256,8]{1,0:T(8,128)} %copy.12.w_ref, ...), custom_call_target="tpu_custom_call" | custom-call | tf_op jit(solution)/shard_map/pallas_call | solution.py:281
  65.4 1.9 %copy.15 = bf16[256,8,128]{2,1,0:T(8,128)(2,1)} copy(bf16[256,8,128]{2,1,0:T(8,128)(2,1)} %bitcast.5) | data formatting | bytes 1048576
  67.2 1.5 %copy.16 = f32[128,128]{1,0:T(8,128)} copy(f32[128,128]{1,0:T(8,128)} %get-tuple-element.9) | data formatting | bytes 131072

commit v2 on v1

v2 whole, which is shorter than its diff:
```python
import functools
import jax
import jax.numpy as jnp
from jax import lax
from jax.experimental import pallas as pl
from jax.experimental.pallas import tpu as pltpu
from jax.sharding import PartitionSpec as P

attn_scale = 192.0 ** (-0.5)
MESH = pl.DeviceIdType.MESH
F32 = jnp.float32
BF16 = jnp.bfloat16


def dot(a, b, ca, cb):
    return lax.dot_general(a, b, (((ca,), (cb,)), ((), ())), preferred_element_type=F32)


def kernel(
    ns, nh, heads, iheads, index_scale, group,
    q_hbm, kl_ref, nrm_ref, iq_hbm, ik_ref, w_ref, kept_ref,
    dq_hbm, dk_ref,
    qbuf, iq_ref, klat, keys, wm, w_col, hacc,
    s1l, r1l, s2l, r2l, s1h, r1h, own_h, s2h, r2h, gall, dz_ref, dq_ref, acc,
    sa, ra, sb, rb, rc,
    q_sem, iq_sem, dq_sem, ik_send, ik_recv, kl_send, kl_recv,
    l1_send, l1_recv, h1_send, h1_recv, l2_send, l2_recv, h2_send, h2_recv,
    g_send, g_fsend, g_recv, a_send, a_recv, b_send, b_recv, c_send, c_recv,
):
    me_s, me_h = lax.axis_index("seq"), lax.axis_index("head")
    half = nh // 2
    mz, mx = me_h // 2, me_h % 2
    px = 1 - mx
    pair = mz * 2 + px
    n_keys, kb = klat.shape[0], ik_ref.shape[0]
    cr = r1l.shape[1]
    hr = cr * half
    wr = cr * iheads
    nb, bk = s1h.shape[0], s1h.shape[2]

    def copy(src, dst, ss, rs, s, h):
        return pltpu.make_async_remote_copy(
            src_ref=src, dst_ref=dst, send_sem=ss, recv_sem=rs,
            device_id=(s, h), device_id_type=MESH,
        )

    iq_copy = pltpu.make_async_copy(iq_hbm, iq_ref, iq_sem)
    iq_copy.start()
    q_parts = q_sem.shape[0]
    qh = heads // q_parts

    def q_copy(i):
        return pltpu.make_async_copy(
            q_hbm.at[pl.ds(i * qh, qh)], qbuf.at[pl.ds(i * qh, qh)], q_sem.at[i]
        )

    for i in range(q_parts):
        q_copy(i).start()

    barrier = pltpu.get_barrier_semaphore()
    for d in range(1, ns):
        pl.semaphore_signal(barrier, inc=1, device_id=((me_s + d) % ns, me_h), device_id_type=MESH)
    for d in range(1, nh):
        pl.semaphore_signal(barrier, inc=1, device_id=(me_s, (me_h + d) % nh), device_id_type=MESH)

    def own_rows(s):
        return pl.ds(pl.multiple_of(s * kb, kb), kb)

    klat[own_rows(me_s), :] = kl_ref[...].T
    keys[own_rows(me_s), :] = ik_ref[...]
    w_col[...] = w_ref[...].T
    pl.semaphore_wait(barrier, ns - 1 + nh - 1)

    def ik_copy(d, s):
        rows = own_rows(s)
        return copy(keys.at[rows], keys.at[rows], ik_send.at[d], ik_recv.at[s], (me_s + d) % ns, me_h)

    def kl_copy(d, s):
        rows = own_rows(s)
        return copy(klat.at[rows], klat.at[rows], kl_send.at[d], kl_recv.at[s], (me_s + d) % ns, me_h)

    for d in range(1, ns):
        ik_copy(d, me_s).start()
    for d in range(1, ns):
        kl_copy(d, me_s).start()
    iq_copy.wait()
    for d in range(1, ns):
        ik_copy(d, (me_s + d) % ns).wait_recv()

    def l1_copy(zt):
        return copy(s1l.at[zt], r1l.at[zt], l1_send.at[zt], l1_recv.at[zt], me_s, pair)

    def l2_copy(zt, frm):
        return copy(s2l.at[zt], r2l.at[frm], l2_send.at[zt], l2_recv.at[frm], me_s, zt * 2 + mx)

    def h1_copy(b):
        return copy(s1h.at[b], r1h.at[b], h1_send.at[b], h1_recv.at[b], me_s, pair)

    def h2_copy(b, zt, frm):
        rows = pl.ds(pl.multiple_of(zt * cr, cr), cr)
        return copy(
            s2h.at[b, rows], r2h.at[frm, b], h2_send.at[b, zt], h2_recv.at[b, frm], me_s, zt * 2 + mx
        )

    def z_step(i, _):
        zt = (mz + 1 + i) % half
        k = jnp.where(i < half, px, mx) * half + zt
        rows = pl.ds(pl.multiple_of(k * cr, cr), cr)
        wide = pl.ds(pl.multiple_of(k * wr, wr), wr)
        z = dot(iq_ref[wide, :], keys[...], 1, 1).reshape(cr, iheads, n_keys)
        wide_w = jnp.broadcast_to(w_col[rows, :][:, None, :], (cr, iheads, iheads))
        sub = lax.broadcasted_iota(jnp.int32, (cr, iheads, iheads), 1)
        lane = lax.broadcasted_iota(jnp.int32, (cr, iheads, iheads), 2)
        w = jnp.sum(jnp.where(sub == lane, wide_w, 0.0), axis=2, keepdims=True)
        part = jnp.where(z > 0, w, 0.0)
        wm[k] = part.reshape(wr, n_keys)
        logit = jnp.sum(part * z, axis=1) * index_scale

        @pl.when(i < half)
        def _():
            s1l[zt] = logit
            l1_copy(zt).start()

        @pl.when(i >= half)
        def _():
            s2l[zt] = logit

        return 0

    lax.fori_loop(0, nh, z_step, 0)

    for d in range(1, ns):
        kl_copy(d, (me_s + d) % ns).wait_recv()
    for i in range(q_parts):
        q_copy(i).wait()

    def half_rows(x):
        return pl.ds(pl.multiple_of(x * hr, hr), hr)

    def pass_logits():
        for d in range(1, half + 1):
            zt = (mz + d) % half
            l1_copy(zt).wait_recv()
            s2l[zt] = s2l[zt] + r1l[zt]
            if d < half:
                l2_copy(zt, mz).start()

    def pass_sums(b):
        h1_copy(b).wait_recv()
        s2h[b] = (own_h[b] + r1h[b].astype(F32)).astype(BF16)
        for d in range(1, half):
            h2_copy(b, (mz + d) % half, mz).start()

    for b in range(nb):
        hacc[...] = jnp.zeros_like(hacc)

        def score_step(i, _):
            total = hacc[...]
            for j in range(group):
                h = i * group + j
                s = dot(klat[b * bk:(b + 1) * bk, :], qbuf[h], 1, 0)
                total = total + jnp.exp(s * attn_scale - nrm_ref[pl.ds(h, 1), :])
            hacc[...] = total
            return 0

        lax.fori_loop(0, heads // group, score_step, 0)
        turned = hacc[...].T
        low, high = turned[:hr], turned[hr:]
        s1h[b] = jnp.where(px == 0, low, high).astype(BF16)
        h1_copy(b).start()
        own_h[b] = jnp.where(mx == 0, low, high)
        if b == 0:
            pass_logits()
        if b > 0:
            pass_sums(b - 1)
    pass_sums(nb - 1)

    logit = s2l[mz]
    for d in range(1, half):
        frm = (mz + half - d) % half
        l2_copy(frm, frm).wait_recv()
        logit = logit + r2l[frm]

    mine = mx * half + mz
    tile_rows = (cr * nh) // kept_ref.shape[0]
    tile_at = (mine * cr) // tile_rows
    kt = n_keys // kept_ref.shape[1]
    keep = jnp.concatenate(
        [jnp.full((cr, kt), kept_ref[tile_at, j], jnp.int32) for j in range(kept_ref.shape[1])],
        axis=1,
    ) > 0
    top = jnp.max(jnp.where(keep, logit, -jnp.inf), axis=1, keepdims=True)
    expo = jnp.where(keep, jnp.exp(jnp.where(keep, logit, top) - top), 0.0)
    iprob = expo / jnp.sum(expo, axis=1, keepdims=True)

    sums = []
    for b in range(nb):
        value = s2h[b, pl.ds(pl.multiple_of(mz * cr, cr), cr)].astype(F32)
        for d in range(1, half):
            frm = (mz + half - d) % half
            h2_copy(b, frm, frm).wait_recv()
            value = value + r2h[frm, b].astype(F32)
        sums.append(value)
    head_sum = jnp.where(keep, jnp.concatenate(sums, axis=1), 0.0)
    target = head_sum / jnp.sum(head_sum, axis=1, keepdims=True)
    gall[mine] = (iprob - target).astype(BF16)

    def g_copy(d, k):
        zt = (mz + d) % half
        return copy(gall.at[k], gall.at[k], g_send.at[d], g_recv.at[k], me_s, zt * 2 + mx)

    def g_pass(d, k):
        return copy(gall.at[k], gall.at[k], g_fsend.at[d], g_recv.at[k], me_s, pair)

    for d in range(1, half):
        g_copy(d, mine).start()
    g_pass(0, mine).start()

    acc[...] = jnp.zeros_like(acc)

    def back_step(i, _):
        zt = (mz + half - i % half) % half
        k = jnp.where(i < half, mx, px) * half + zt

        @pl.when(jnp.logical_and(i > 0, i < half))
        def _():
            g_copy(i, k).wait_recv()
            g_pass(i, k).start()

        @pl.when(i >= half)
        def _():
            g_pass(i - half, k).wait_recv()

        wide = pl.ds(pl.multiple_of(k * wr, wr), wr)
        g = gall[k].astype(F32)
        dz = (g[:, None, :] * wm[k].reshape(cr, iheads, n_keys)).astype(BF16).reshape(wr, n_keys)
        dz_ref[wide, :] = dz
        acc[...] += dot(iq_ref[wide, :], dz, 0, 0)
        return 0

    lax.fori_loop(0, nh, back_step, 0)

    wire = sb.dtype
    br = rb.shape[1]

    def a_copy(d, s):
        return copy(sa.at[d], ra.at[s], a_send.at[d], a_recv.at[s], (me_s + d) % ns, me_h)

    for d in range(1, ns):
        sa[d] = (acc[:, own_rows((me_s + d) % ns)] * index_scale).astype(BF16)
        a_copy(d, me_s).start()

    def dq_copy(i):
        wide = pl.ds(i * wr, wr)
        return pltpu.make_async_copy(dq_ref.at[wide], dq_hbm.at[wide], dq_sem.at[i])

    def dq_step(i, _):
        wide = pl.ds(pl.multiple_of(i * wr, wr), wr)
        dq_ref[wide, :] = (dot(dz_ref[wide, :], keys[...], 1, 0) * index_scale).astype(BF16)
        dq_copy(i).start()
        return 0

    lax.fori_loop(0, half, dq_step, 0)

    total = acc[:, own_rows(me_s)] * index_scale
    for d in range(1, ns):
        a_copy(d, (me_s + d) % ns).wait_recv()
        total = total + ra[(me_s + d) % ns].astype(F32)
    sb[...] = total.astype(wire)

    def b_rows(h):
        return pl.ds(pl.multiple_of(h * br, br), br)

    def b_copy(d, h):
        to = (me_h + d) % nh
        return copy(sb.at[b_rows(to)], rb.at[h], b_send.at[d], b_recv.at[h], me_s, to)

    def c_copy(d, h):
        return copy(rc.at[b_rows(h)], rc.at[b_rows(h)], c_send.at[d], c_recv.at[h], me_s, (me_h + d) % nh)

    for d in range(1, nh):
        b_copy(d, me_h).start()

    lax.fori_loop(half, nh, dq_step, 0)

    piece = sb[b_rows(me_h), :].astype(F32)
    for d in range(1, nh):
        frm = (me_h + d) % nh
        b_copy(d, frm).wait_recv()
        piece = piece + rb[frm].astype(F32)
    rc[b_rows(me_h), :] = piece.astype(wire)
    for d in range(1, nh):
        c_copy(d, me_h).start()
    for d in range(1, nh):
        c_copy(d, (me_h + d) % nh).wait_recv()
    dk_ref[...] = rc[...].astype(F32).T

    for i in range(nh):
        dq_copy(i).wait()
    for d in range(1, ns):
        ik_copy(d, me_s).wait_send()
        kl_copy(d, me_s).wait_send()
        a_copy(d, me_s).wait_send()
    for i in range(half):
        l1_copy(i).wait_send()
        g_pass(i, mine).wait_send()
    for b in range(nb):
        h1_copy(b).wait_send()
    for d in range(1, half):
        zt = (mz + d) % half
        l2_copy(zt, mz).wait_send()
        g_copy(d, mine).wait_send()
        for b in range(nb):
            h2_copy(b, zt, mz).wait_send()
    for d in range(1, nh):
        b_copy(d, me_h).wait_send()
        c_copy(d, me_h).wait_send()


def local(ns, nh, query_latent, key_latent, normalizer, index_query, index_key, index_weight, kept):
    t, heads, width = query_latent.shape
    ihead, idim = index_query.shape[1:]
    iheads = -(-ihead // 8) * 8
    if iheads != ihead:
        index_query = jnp.pad(index_query, ((0, 0), (0, iheads - ihead), (0, 0)))
        index_weight = jnp.pad(index_weight, ((0, 0), (0, iheads - ihead)))
    kb = key_latent.shape[0]
    n_keys = kb * ns
    cr, half, br = t // nh, nh // 2, idim // nh
    wire = BF16 if br % 16 == 0 else F32
    bk = 2 * kb
    nb = n_keys // bk
    group = 4 if heads % 4 == 0 else 1
    parts = 4 if heads % 4 == 0 else 1
    vmem, dma = pltpu.VMEM, pltpu.SemaphoreType.DMA
    in_vmem, in_hbm = pl.BlockSpec(memory_space=pltpu.VMEM), pl.BlockSpec(memory_space=pl.ANY)
    dq, dk = pl.pallas_call(
        functools.partial(kernel, ns, nh, heads, iheads, idim ** (-0.5), group),
        out_shape=(
            jax.ShapeDtypeStruct((t * iheads, idim), BF16),
            jax.ShapeDtypeStruct((kb, idim), F32),
        ),
        in_specs=[in_hbm, in_vmem, in_vmem, in_hbm, in_vmem, in_vmem,
                  pl.BlockSpec(memory_space=pltpu.SMEM)],
        out_specs=(in_hbm, in_vmem),
        scratch_shapes=[
            vmem((heads, width, t), BF16),
            vmem((t * iheads, idim), BF16),
            vmem((n_keys, width), BF16),
            vmem((n_keys, idim), BF16),
            vmem((nh, cr * iheads, n_keys), F32),
            vmem((t, iheads), F32),
            vmem((bk, t), F32),
            vmem((half, cr, n_keys), F32),
            vmem((half, cr, n_keys), F32),
            vmem((half, cr, n_keys), F32),
            vmem((half, cr, n_keys), F32),
            vmem((nb, t // 2, bk), BF16),
            vmem((nb, t // 2, bk), BF16),
            vmem((nb, t // 2, bk), F32),
            vmem((nb, t // 2, bk), BF16),
            vmem((half, nb, cr, bk), BF16),
            vmem((nh, cr, n_keys), BF16),
            vmem((t * iheads, n_keys), BF16),
            vmem((t * iheads, idim), BF16),
            vmem((idim, n_keys), F32),
            vmem((ns, idim, kb), BF16),
            vmem((ns, idim, kb), BF16),
            vmem((idim, kb), wire),
            vmem((nh, br, kb), wire),
            vmem((idim, kb), wire),
            dma((parts,)), dma, dma((nh,)), dma((ns,)), dma((ns,)), dma((ns,)), dma((ns,)),
            dma((half,)), dma((half,)), dma((nb,)), dma((nb,)),
            dma((half,)), dma((half,)), dma((nb, half)), dma((nb, half)),
            dma((half,)), dma((half,)), dma((nh,)),
            dma((ns,)), dma((ns,)), dma((nh,)), dma((nh,)), dma((nh,)), dma((nh,)),
        ],
        compiler_params=pltpu.CompilerParams(
            collective_id=0, has_side_effects=True, vmem_limit_bytes=60 * 1024 * 1024
        ),
    )(
        query_latent.transpose(1, 2, 0), key_latent.T, normalizer.T,
        index_query.reshape(t * iheads, idim), index_key, index_weight.T, kept,
    )
    dq = dq.reshape(t, iheads, idim)
    return (dq[:, :ihead] if iheads != ihead else dq), dk


def solution(mesh):
    ns, nh = mesh.shape["seq"], mesh.shape["head"]
    return jax.shard_map(
        functools.partial(local, ns, nh),
        mesh=mesh,
        in_specs=(
            P("seq", "head", None),
            P("seq", None),
            P("seq", "head"),
            P("seq", "head", None),
            P("seq", None),
            P("seq", "head"),
            P("seq", None),
        ),
        out_specs=(P("seq", "head", None), P("seq", None)),
        check_vma=False,
    )
```

time: 69.2 us -> 53.4 us (0.77)
  local copies, waits for them, and re-layouts: 16.9 us -> 3.34 us
  Pallas kernels: 51.2 us -> 49.2 us
    unnamed x6 -> x2, local copies, waits for them, and re-layouts: 16.9 us -> 3.34 us
    pallas_call x1, Pallas kernels: 51.2 us -> 49.2 us  [local(): pl.pallas_call(functools.partial(kernel, ns, nh, heads, iheads, idim ** (...]
where the time goes in v2:
time: 53.4 us; the launch traced here: 53.2 us
  Pallas kernels  49.2 us (92%)
  local copies, waits for them, and re-layouts  3.34 us (6%)
  between operations  0.64 us (1%)
    pallas_call x1, Pallas kernels, local(): pl.pallas_call(functools.partial(kernel, ns, nh, heads, iheads, idim ** (...  49.2 us
    unnamed x2, local copies, waits for them, and re-layouts  3.34 us

profile of v2, /device:TPU:0, one launch (start us, length us, event | category | flops | bytes accessed | tf_op | source)
XLA Modules:
  0.0 53.2 jit_solution(4094703667357202134)
XLA Ops:
  0.6 49.2 %shard_map.86 = (bf16[2048,128]{1,0:T(8,128)(2,1)}, f32[128,128]{1,0:T(8,128)}) custom-call(bf16[16,576,256]{2,1,0:T(8,128)(2,1)} %bitcast.6, bf16[576,128]{1,0:T(8,128)(2,1)} %bitcast.9, f32[16,256]{1,0:T(8,128)} %bitcast.10, bf16[2048,128]{1,0:T(8,128)(2,1)} %bitcast.7, bf16[128,128]{1,0:T(8,128)(2,1)} %ik_ref.1, f32[8,256]{1,0:T(8,128)} %bitcast.11, ...), custom_call_target="tpu_custom_call" | custom-call | tf_op jit(solution)/shard_map/pallas_call | solution.py:337
  49.8 1.9 %copy.11 = bf16[256,8,128]{2,1,0:T(8,128)(2,1)} copy(bf16[256,8,128]{2,1,0:T(8,128)(2,1)} %bitcast.8) | data formatting | bytes 1048576
  51.7 1.5 %copy.12 = f32[128,128]{1,0:T(8,128)} copy(f32[128,128]{1,0:T(8,128)} %get-tuple-element.9) | data formatting | bytes 131072

commit v3 on v2

--- a/solution.py
+++ b/solution.py
@@ -18,12 +18,12 @@
 
 def kernel(
     ns, nh, heads, iheads, index_scale, group,
-    q_hbm, kl_ref, nrm_ref, iq_hbm, ik_ref, w_ref, kept_ref,
+    q_hbm, kl_hbm, nrm_hbm, iq_hbm, ik_hbm, w_hbm, kept_ref,
     dq_hbm, dk_ref,
-    qbuf, iq_ref, klat, keys, wm, w_col, hacc,
+    nrm_ref, w_ref, klt, qbuf, iq_ref, klat, keys, wm, w_col, hacc,
     s1l, r1l, s2l, r2l, s1h, r1h, own_h, s2h, r2h, gall, dz_ref, dq_ref, acc,
     sa, ra, sb, rb, rc,
-    q_sem, iq_sem, dq_sem, ik_send, ik_recv, kl_send, kl_recv,
+    q_sem, iq_sem, in_sem, dq_sem, ik_send, ik_recv, kl_send, kl_fsend, kl_recv,
     l1_send, l1_recv, h1_send, h1_recv, l2_send, l2_recv, h2_send, h2_recv,
     g_send, g_fsend, g_recv, a_send, a_recv, b_send, b_recv, c_send, c_recv,
 ):
@@ -32,7 +32,7 @@
     mz, mx = me_h // 2, me_h % 2
     px = 1 - mx
     pair = mz * 2 + px
-    n_keys, kb = klat.shape[0], ik_ref.shape[0]
+    n_keys, kb = klat.shape[0], ik_hbm.shape[0]
     cr = r1l.shape[1]
     hr = cr * half
     wr = cr * iheads
@@ -44,8 +44,25 @@
             device_id=(s, h), device_id_type=MESH,
         )
 
+    barrier = pltpu.get_barrier_semaphore()
+    for d in range(1, ns):
+        pl.semaphore_signal(barrier, inc=1, device_id=((me_s + d) % ns, me_h), device_id_type=MESH)
+    for d in range(1, nh):
+        pl.semaphore_signal(barrier, inc=1, device_id=(me_s, (me_h + d) % nh), device_id_type=MESH)
+
+    def own_rows(s):
+        return pl.ds(pl.multiple_of(s * kb, kb), kb)
+
+    ik_own = pltpu.make_async_copy(ik_hbm, keys.at[own_rows(me_s)], in_sem.at[0])
+    w_copy = pltpu.make_async_copy(w_hbm, w_ref, in_sem.at[1])
+    kl_own = pltpu.make_async_copy(kl_hbm, klt.at[me_s], in_sem.at[2])
+    nrm_copy = pltpu.make_async_copy(nrm_hbm, nrm_ref, in_sem.at[3])
     iq_copy = pltpu.make_async_copy(iq_hbm, iq_ref, iq_sem)
+    ik_own.start()
+    w_copy.start()
     iq_copy.start()
+    kl_own.start()
+    nrm_copy.start()
     q_parts = q_sem.shape[0]
     qh = heads // q_parts
 
@@ -56,33 +73,32 @@
 
     for i in range(q_parts):
         q_copy(i).start()
-
-    barrier = pltpu.get_barrier_semaphore()
-    for d in range(1, ns):
-        pl.semaphore_signal(barrier, inc=1, device_id=((me_s + d) % ns, me_h), device_id_type=MESH)
-    for d in range(1, nh):
-        pl.semaphore_signal(barrier, inc=1, device_id=(me_s, (me_h + d) % nh), device_id_type=MESH)
-
-    def own_rows(s):
-        return pl.ds(pl.multiple_of(s * kb, kb), kb)
-
-    klat[own_rows(me_s), :] = kl_ref[...].T
-    keys[own_rows(me_s), :] = ik_ref[...]
+    pl.semaphore_wait(barrier, ns - 1 + nh - 1)
+
+    chips = ns // 2
+    mp, mc = me_s // 2, me_s % 2
+    other = mp * 2 + 1 - mc
+
+    def ik_copy(d, s):
+        return copy(ik_hbm, keys.at[own_rows(s)], ik_send.at[d], ik_recv.at[s], (me_s + d) % ns, me_h)
+
+    def kl_copy(d, s):
+        return copy(kl_hbm, klt.at[s], kl_send.at[d], kl_recv.at[s], ((mp + d) % chips) * 2 + mc, me_h)
+
+    def kl_pair(s):
+        return copy(kl_hbm, klt.at[s], kl_send.at[0], kl_recv.at[s], other, me_h)
+
+    def kl_pass(d, s):
+        return copy(klt.at[s], klt.at[s], kl_fsend.at[d], kl_recv.at[s], other, me_h)
+
+    for d in range(1, ns):
+        ik_copy(d, me_s).start()
+    for d in range(1, chips):
+        kl_copy(d, me_s).start()
+    kl_pair(me_s).start()
+    ik_own.wait()
+    w_copy.wait()
     w_col[...] = w_ref[...].T
-    pl.semaphore_wait(barrier, ns - 1 + nh - 1)
-
-    def ik_copy(d, s):
-        rows = own_rows(s)
-        return copy(keys.at[rows], keys.at[rows], ik_send.at[d], ik_recv.at[s], (me_s + d) % ns, me_h)
-
-    def kl_copy(d, s):
-        rows = own_rows(s)
-        return copy(klat.at[rows], klat.at[rows], kl_send.at[d], kl_recv.at[s], (me_s + d) % ns, me_h)
-
-    for d in range(1, ns):
-        ik_copy(d, me_s).start()
-    for d in range(1, ns):
-        kl_copy(d, me_s).start()
     iq_copy.wait()
     for d in range(1, ns):
         ik_copy(d, (me_s + d) % ns).wait_recv()
@@ -127,10 +143,22 @@
 
         return 0
 
-    lax.fori_loop(0, nh, z_step, 0)
-
-    for d in range(1, ns):
-        kl_copy(d, (me_s + d) % ns).wait_recv()
+    lax.fori_loop(0, half, z_step, 0)
+    for d in range(1, chips):
+        frm = ((mp + d) % chips) * 2 + mc
+        kl_copy(d, frm).wait_recv()
+        kl_pass(d, frm).start()
+    lax.fori_loop(half, nh, z_step, 0)
+
+    kl_own.wait()
+    nrm_copy.wait()
+    for d in range(chips):
+        here = ((mp + d) % chips) * 2 + mc
+        klat[own_rows(here), :] = klt[here].T
+    for d in range(chips):
+        there = ((mp + d) % chips) * 2 + 1 - mc
+        kl_pass(d, there).wait_recv()
+        klat[own_rows(there), :] = klt[there].T
     for i in range(q_parts):
         q_copy(i).wait()
 
@@ -299,8 +327,11 @@
         dq_copy(i).wait()
     for d in range(1, ns):
         ik_copy(d, me_s).wait_send()
+        a_copy(d, me_s).wait_send()
+    kl_pair(me_s).wait_send()
+    for d in range(1, chips):
         kl_copy(d, me_s).wait_send()
-        a_copy(d, me_s).wait_send()
+        kl_pass(d, me_s).wait_send()
     for i in range(half):
         l1_copy(i).wait_send()
         g_pass(i, mine).wait_send()
@@ -315,6 +346,15 @@
     for d in range(1, nh):
         b_copy(d, me_h).wait_send()
         c_copy(d, me_h).wait_send()
+
+
+def hand_over(dq_in, dk_in, dq_out, dk_out, sem):
+    first = pltpu.make_async_copy(dq_in, dq_out, sem.at[0])
+    second = pltpu.make_async_copy(dk_in, dk_out, sem.at[1])
+    first.start()
+    second.start()
+    first.wait()
+    second.wait()
 
 
 def local(ns, nh, query_latent, key_latent, normalizer, index_query, index_key, index_weight, kept):
@@ -340,10 +380,12 @@
             jax.ShapeDtypeStruct((t * iheads, idim), BF16),
             jax.ShapeDtypeStruct((kb, idim), F32),
         ),
-        in_specs=[in_hbm, in_vmem, in_vmem, in_hbm, in_vmem, in_vmem,
-                  pl.BlockSpec(memory_space=pltpu.SMEM)],
+        in_specs=[in_hbm] * 6 + [pl.BlockSpec(memory_space=pltpu.SMEM)],
         out_specs=(in_hbm, in_vmem),
         scratch_shapes=[
+            vmem((heads, t), F32),
+            vmem((iheads, t), F32),
+            vmem((ns, width, kb), BF16),
             vmem((heads, width, t), BF16),
             vmem((t * iheads, idim), BF16),
             vmem((n_keys, width), BF16),
@@ -369,7 +411,8 @@
             vmem((idim, kb), wire),
             vmem((nh, br, kb), wire),
             vmem((idim, kb), wire),
-            dma((parts,)), dma, dma((nh,)), dma((ns,)), dma((ns,)), dma((ns,)), dma((ns,)),
+            dma((parts,)), dma, dma((4,)), dma((nh,)), dma((ns,)), dma((ns,)),
+            dma((ns // 2,)), dma((ns // 2,)), dma((ns,)),
             dma((half,)), dma((half,)), dma((nb,)), dma((nb,)),
             dma((half,)), dma((half,)), dma((nb, half)), dma((nb, half)),
             dma((half,)), dma((half,)), dma((nh,)),
@@ -382,6 +425,16 @@
         query_latent.transpose(1, 2, 0), key_latent.T, normalizer.T,
         index_query.reshape(t * iheads, idim), index_key, index_weight.T, kept,
     )
+    dq, dk = pl.pallas_call(
+        hand_over,
+        out_shape=(
+            jax.ShapeDtypeStruct((t * iheads, idim), BF16),
+            jax.ShapeDtypeStruct((kb, idim), F32),
+        ),
+        in_specs=[in_hbm] * 2,
+        out_specs=(in_hbm, in_hbm),
+        scratch_shapes=[dma((2,))],
+    )(dq, dk)
     dq = dq.reshape(t, iheads, idim)
     return (dq[:, :ihead] if iheads != ihead else dq), dk
 

time: 53.4 us -> 68.5 us (1.28)
  Pallas kernels: 49.2 us -> 67.7 us
  local copies, waits for them, and re-layouts: 3.34 us -> 0 us
    pallas_call x0 -> x1, Pallas kernels: none -> 19 us  [local(): pl.pallas_call(hand_over, out_shape=(jax.ShapeDtypeStruct((t * iheads, id...]
    unnamed x2 -> x0, local copies, waits for them, and re-layouts: 3.34 us -> none
where the time goes in v3:
time: 68.5 us; the launch traced here: 68.3 us
  Pallas kernels  67.7 us (99%)
    pallas_call x1, Pallas kernels, local(): pl.pallas_call(functools.partial(kernel, ns, nh, heads, iheads, idim ** (...  48.7 us
    pallas_call x1, Pallas kernels, local(): pl.pallas_call(hand_over, out_shape=(jax.ShapeDtypeStruct((t * iheads, id...  19 us

profile of v3, /device:TPU:0, one launch (start us, length us, event | category | flops | bytes accessed | tf_op | source)
XLA Modules:
  0.0 68.3 jit_solution(17032830825809312172)
XLA Ops:
  0.6 48.7 %shard_map.86 = (bf16[2048,128]{1,0:T(8,128)(2,1)}, f32[128,128]{1,0:T(8,128)}) custom-call(bf16[16,576,256]{2,1,0:T(8,128)(2,1)} %bitcast.6, bf16[576,128]{1,0:T(8,128)(2,1)} %bitcast.8, f32[16,256]{1,0:T(8,128)} %bitcast.9, bf16[2048,128]{1,0:T(8,128)(2,1)} %bitcast.7, bf16[128,128]{1,0:T(8,128)(2,1)} %ik_hbm.1, f32[8,256]{1,0:T(8,128)} %bitcast.10, ...), custom_call_target="tpu_custom_call" | custom-call | tf_op jit(solution)/shard_map/pallas_call | solution.py:377
  49.4 19.0 %shard_map.87 = (bf16[2048,128]{1,0:T(8,128)(2,1)}, f32[128,128]{1,0:T(8,128)}) custom-call(bf16[2048,128]{1,0:T(8,128)(2,1)} %get-tuple-element.6.dq_in, f32[128,128]{1,0:T(8,128)} %get-tuple-element.7.dk_in), custom_call_target="tpu_custom_call" | custom-call | tf_op jit(solution)/shard_map/pallas_call | solution.py:428
